TPU v7x, 512 devices: a whole 4x8x8 slice. The times are simulated.
512 devices in a mesh: slab: 64 (over x, z, core), dp: 8 (over y).
Axes of the slice: x: 4, y: 8, z: 8, core: 2. Of those that a mesh axis runs over, the one named last changes fastest.
Arguments:
- point_feats: float32 [8, 32768, 128], P('dp', 'slab'), may hold values from -6 to 6
- owner_slab: int32 [8, 32768, 1], P('dp', 'slab'), may hold values from 0 to 63; in each aligned block of 512 rows (0 to 511, 512 to 1023, ..., all dimensions but the last counted through in order) at most 16 rows name the same one
- block_slot: int32 [8, 32768], P('dp', 'slab'), may hold values from 0 to 1
- voxel_index: int32 [8, 32768], P('dp', 'slab'), may hold values from 0 to 511
- boundary: int32 [8, 64, 2, 1], P('dp', 'slab'), may hold values from 0 to 1, as said below
- neighbours: int32 [8, 128, 27], P('dp', 'slab'), may hold values from 0 to 4, as said below
- weight_taps: float32 [27, 128, 128], replicated, may hold values from -0.109375 to 0.109375
- cotangent: float32 [8, 65536, 128], P('dp', 'slab'), may hold values from -6 to 6
Outputs:
- activated: float32 [8, 65536, 128], P('dp', 'slab')
- point_grads: float32 [8, 32768, 128], P('dp', 'slab')
- weight_grads: float32 [3456, 128], P('slab')
Inputs may be any that keep to these rules, and one draw needn't show every extreme that they name: `owner_slab`: among the points of one device, no slab is named by more than 16 points, and exactly 16 in some device. `boundary`: each list of one slab holds 1 different block slots. `neighbours`: entry 13 of a block's row is the block's own slot. Entries 0 to 8 name a block of the slab (below 2), one of the 1 block from the slab before (2 to 2), or the zero block 4; entries 18 to 26 a block of the slab, one of the 1 block from the slab after, or the zero block; the others a block of the slab or the zero block.
All inputs are finite; a program needn't handle non-finite values.
Results may differ from a plain program's by a relative error of at most 0.0003.
Values sent between devices are 32-bit elements; how exact they have to be, the bound alone decides.
A program may use at most 64 MiB of HBM per device.

v0:
```python
import math
import jax
import jax.numpy as jnp
import numpy as np
from jax import lax
from jax.sharding import PartitionSpec as P

C = 128
E = 8
NB = 2
NH = 1
P_DEV = 512
VOX = 512
highest = lax.Precision.HIGHEST


def padded_2(value, sides, width):
    for axis, dim in sides:
        size, length = (lax.axis_size(axis), value.shape[dim])
        up = [(i, (i + 1) % size) for i in range(size)]
        down = [(j, i) for i, j in up]
        last = lax.slice_in_dim(value, length - width, length, axis=dim)
        leading = lax.slice_in_dim(value, 0, width, axis=dim)
        before = lax.ppermute(last, axis, up)
        after = lax.ppermute(leading, axis, down)
        value = jnp.concatenate([before, value, after], axis=dim)
    return value


def grid_tables():
    padded_edge = E + 2
    position = np.arange(padded_edge)
    section = np.where(position == 0, 0, np.where(position == padded_edge - 1, 2, 1))
    within = np.where(position == 0, E - 1, np.where(position == padded_edge - 1, 0, position - 1))
    grid_x, grid_y, grid_z = np.meshgrid(position, position, position, indexing="ij")
    tap_table = section[grid_x] * 9 + section[grid_y] * 3 + section[grid_z]
    voxel_table = within[grid_x] * E * E + within[grid_y] * E + within[grid_z]
    return (
        jnp.asarray(tap_table.reshape(-1), jnp.int32),
        jnp.asarray(voxel_table.reshape(-1), jnp.int32),
    )


def column_block(padded, tap_x):
    parts_list = [
        padded[:, tap_x : tap_x + E, tap_y : tap_y + E, tap_z : tap_z + E]
        for tap_y in range(3)
        for tap_z in range(3)
    ]
    return jnp.concatenate(parts_list, axis=-1).reshape(NB * VOX, 9 * C)


def per_device(
    point_feats, owner_slab, block_slot, voxel_index, boundary, neighbours, weight_taps, cotangent
):
    slabs = lax.axis_size("slab")
    windows = lax.axis_size("dp")
    capacity = 2 * P_DEV // slabs
    features = point_feats[0]
    target = owner_slab[0, :, 0]
    onehot = (target[:, None] == jnp.arange(slabs)[None, :]).astype(jnp.int32)
    ranks = jnp.sum((jnp.cumsum(onehot, axis=0) - onehot) * onehot, axis=1)
    placement = target * capacity + ranks
    send_rows = jnp.zeros((slabs * capacity, C), jnp.float32).at[placement].set(features)
    send_ids = (
        jnp.full((slabs * capacity,), -1, jnp.int32)
        .at[placement]
        .set(block_slot[0] * VOX + voxel_index[0])
    )
    recv_rows, recv_ids = (
        lax.all_to_all(
            send_rows.reshape(slabs, capacity, C), "slab", split_axis=0, concat_axis=0, tiled=True
        ),
        lax.all_to_all(
            send_ids.reshape(slabs, capacity), "slab", split_axis=0, concat_axis=0, tiled=True
        ),
    )
    flat_ids = recv_ids.reshape(-1)
    target_rows = jnp.where(flat_ids < 0, NB * VOX, flat_ids)
    voxel_feats = (
        jnp.zeros((NB * VOX + 1, C), jnp.float32)
        .at[target_rows]
        .add(recv_rows.reshape(-1, C))[: NB * VOX]
    )
    blocks = voxel_feats.reshape(NB, VOX, C)
    lend_left = boundary[0, 0, 0]
    lend_right = boundary[0, 0, 1]
    sent_left = blocks[lend_left]
    sent_right = blocks[lend_right]
    arrived = padded_2(jnp.stack((sent_left, sent_right)), (("slab", 0),), 1)
    from_left = arrived[0]
    from_right = arrived[3]
    slots_all = NB + 2 * NH + 1
    visible = jnp.concatenate(
        [blocks, from_left, from_right, jnp.zeros((1, VOX, C), jnp.float32)], axis=0
    )
    flat_visible = visible.reshape(slots_all * VOX, C)
    tap_table, voxel_table = grid_tables()
    gather_rows = neighbours[0][:, tap_table] * VOX + voxel_table[None, :]
    padded = flat_visible[gather_rows].reshape(NB, E + 2, E + 2, E + 2, C)
    pre_act = jnp.zeros((NB * VOX, C), jnp.float32)
    for tap_x in range(3):
        columns = column_block(padded, tap_x)
        group_weight = weight_taps[tap_x * 9 : tap_x * 9 + 9].reshape(9 * C, C)
        pre_act = pre_act + jnp.dot(
            columns, group_weight, precision=highest, preferred_element_type=jnp.float32
        )
    gate_value = jax.nn.sigmoid(pre_act)
    activated = pre_act * gate_value
    grad_pre = cotangent[0] * gate_value * (1.0 + pre_act * (1.0 - gate_value))
    pieces = []
    back_groups = []
    for tap_x in range(3):
        columns = column_block(padded, tap_x)
        pieces.append(
            lax.dot_general(
                columns,
                grad_pre,
                (((0,), (0,)), ((), ())),
                precision=highest,
                preferred_element_type=jnp.float32,
            )
        )
        group_back = weight_taps[tap_x * 9 : tap_x * 9 + 9].transpose(2, 0, 1).reshape(C, 9 * C)
        back_groups.append(
            jnp.dot(
                grad_pre, group_back, precision=highest, preferred_element_type=jnp.float32
            ).reshape(NB, E, E, E, 9, C)
        )
    weight_term = jnp.concatenate(pieces, axis=0)
    grad_padded = jnp.zeros((NB, E + 2, E + 2, E + 2, C), jnp.float32)
    for tap_x in range(3):
        for tap_y in range(3):
            for tap_z in range(3):
                shifted = back_groups[tap_x][:, :, :, :, tap_y * 3 + tap_z]
                grad_padded = grad_padded + jnp.pad(
                    shifted,
                    ((0, 0), (tap_x, 2 - tap_x), (tap_y, 2 - tap_y), (tap_z, 2 - tap_z), (0, 0)),
                )
    grad_visible = (
        jnp.zeros((slots_all * VOX, C), jnp.float32)
        .at[gather_rows.reshape(-1)]
        .add(grad_padded.reshape(-1, C))
    )
    grad_visible = grad_visible.reshape(slots_all, VOX, C)
    left_grads = grad_visible[NB : NB + NH]
    right_grads = grad_visible[NB + NH : NB + 2 * NH]
    returned = padded_2(jnp.stack((left_grads, right_grads)), (("slab", 0),), 1)
    for_lent_left = returned[0]
    for_lent_right = returned[3]
    grad_blocks = (
        grad_visible[:NB].at[lend_left].add(for_lent_left).at[lend_right].add(for_lent_right)
    )
    grad_flat = jnp.concatenate(
        [grad_blocks.reshape(NB * VOX, C), jnp.zeros((1, C), jnp.float32)], axis=0
    )
    back_points = grad_flat[target_rows].reshape(slabs, capacity, C)
    came_back = lax.all_to_all(back_points, "slab", split_axis=0, concat_axis=0, tiled=True)
    point_grads = came_back.reshape(slabs * capacity, C)[placement]
    share = lax.psum_scatter(weight_term, "slab", scatter_dimension=0, tiled=True)
    total = lax.psum(share, "dp")
    scale = 1.0 / math.sqrt(windows * slabs * NB * VOX)
    return (activated[None], point_grads[None], total * scale)


def solution(mesh):
    return jax.shard_map(
        per_device,
        mesh=mesh,
        in_specs=(
            P("dp", "slab", None),
            P("dp", "slab", None),
            P("dp", "slab"),
            P("dp", "slab"),
            P("dp", "slab", None, None),
            P("dp", "slab", None),
            P(),
            P("dp", "slab", None),
        ),
        out_specs=(P("dp", "slab", None), P("dp", "slab", None), P("slab", None)),
        check_vma=False,
    )
```

profile of v0, /device:TPU:4, one launch (start us, length us, event | category | flops | bytes accessed | tf_op | source)
XLA Modules:
  0.0 403.9 jit_solution(14868015423676881469)
XLA Ops:
  0.7 0.7 fusion.20
  1.4 1.2 reduce-window.6
  2.9 0.8 fusion.19
  3.7 0.7 compare_select_fusion.4
  4.4 0.7 multiply_add_fusion
  5.1 2.4 scatter_custom_fusion
  7.5 0.7 all_to_all.12
  8.2 13.9 %all-to-all-start = ((s32[64,1,16]{2,1,0:T(1,128)}), s32[64,1,16]{2,1,0:T(1,128)S(1)}, u32[]{:S(2)}, u32[]{:S(2)}) async-start(s32[64,1,16]{2,1,0:T(1,128)} %bitcast.7), calls=%async_computation | async-start | bytes 65536 | tf_op jit(solution)/shard_map/all_to_all | solution.py:74
  22.2 1.3 fusion.27
  26.1 2.7 fusion.26
  30.0 1.5 and_reduce_fusion
  31.5 0.8 copy.103
  32.3 2.5 scatter_custom_fusion.1
  34.9 10.3 %all-to-all-start.1 = ((f32[64,16,128]{2,1,0:T(8,128)}), f32[64,16,128]{2,1,0:T(8,128)S(1)}, u32[]{:S(2)}, u32[]{:S(2)}) async-start(f32[64,16,128]{2,1,0:T(8,128)} %bitcast.10), calls=%async_computation.1 | async-start | bytes 1048576 | tf_op jit(solution)/shard_map/all_to_all | solution.py:71
  45.7 0.7 reduce.21
  46.6 2.9 gather_fusion
  49.8 12.1 %all-to-all-done.1 = f32[64,16,128]{2,1,0:T(8,128)S(1)} async-done(((f32[64,16,128]{2,1,0:T(8,128)}), f32[64,16,128]{2,1,0:T(8,128)S(1)}, u32[]{:S(2)}, u32[]{:S(2)}) %all-to-all-start.1) | async-done | bytes 524320 | tf_op jit(solution)/shard_map/all_to_all | solution.py:71
  61.9 6.2 %scatter_custom_fusion.2 = f32[1025,128]{1,0:T(8,128)S(1)} fusion(s32[1024]{0:T(1024)S(1)} %bitcast.239, f32[1024,128]{1,0:T(8,128)S(1)} %bitcast.232, f32[]{:T(128)} %constant.74.clone.1), kind=kCustom, calls=%fused_computation.81 | custom fusion | flops 131072 | bytes 524804 | tf_op jit(solution)/shard_map/scatter-add | solution.py:83
  68.2 2.5 collective-permute-start
  70.6 5.2 %collective-permute-start.1 = (f32[1,1,512,128]{3,2,1,0:T(8,128)S(1)}, f32[1,1,512,128]{3,2,1,0:T(8,128)S(1)}, u32[]{:S(2)}, u32[]{:S(2)}) collective-permute-start(f32[1,1,512,128]{3,2,1,0:T(8,128)S(1)} %get-tuple-element.113), channel_id=1, source_target_pairs={{8,0},{16,8},{24,16},{32,24},{40,32},{48,40},{56,48},{64,56},{72,6... | collective-permute-start | bytes 786440 | tf_op jit(solution)/shard_map/ppermute | solution.py:25
  76.0 2.0 collective-permute-done
  78.0 1.8 collective-permute-done.1
  79.9 5.8 %gather_fusion.1 = f32[2000,128]{1,0:T(8,128)S(1)} fusion(f32[2560,128]{1,0:T(8,128)S(1)} %bitcast.213, s32[2048]{0:T(1024)S(1)} %pad_clamp_fusion), kind=kCustom, calls=%fused_computation.1 | custom fusion | bytes 2056000 | tf_op jit(solution)/shard_map/gather | solution.py:100
  88.1 4.1 %fusion.28 = f32[1024,128]{1,0:T(8,128)S(1)} fusion(f32[1024,1152]{1,0:T(8,128)S(1)} %bitcast.221, f32[1152,128]{1,0:T(8,128)S(1)} %bitcast.230), kind=kOutput, calls=%fused_computation.130 | convolution fusion | flops 1811939328 | bytes 5832704 | tf_op jit(solution)/shard_map/dot_general | solution.py:105
  92.2 4.1 %convolution_add_fusion.1 = f32[1024,128]{1,0:T(8,128)S(1)} fusion(f32[1024,128]{1,0:T(8,128)S(1)} %fusion.28, f32[1024,1152]{1,0:T(8,128)S(1)} %bitcast.219, f32[1152,128]{1,0:T(8,128)S(1)} %bitcast.229), kind=kOutput, calls=%fused_computation.12 | convolution fusion | flops 1812070400 | bytes 6356992 | tf_op jit(solution)/shard_map/dot_general | solution.py:105
  96.3 5.4 %fusion.9 = (f32[1024,128]{1,0:T(8,128)S(1)}, f32[1,1024,128]{2,1,0:T(8,128)}) fusion(f32[1,1024,128]{2,1,0:T(8,128)S(1)} %copy-done.7, f32[1024,128]{1,0:T(8,128)S(1)} %convolution_add_fusion.1, f32[1024,1152]{1,0:T(8,128)S(1)} %bitcast.217, f32[1152,128]{1,0:T(8,128)S(1)} %bitcast.228), kind=kOutput, calls=%fused_computation.76 | convolution fusion | flops 1813250048 | bytes 7405568 | tf_op jit(solution)/shard_map/dot_general | solution.py:105
  101.7 7.7 %fusion.29 = f32[1152,128]{1,0:T(8,128)S(1)} fusion(f32[1024,1152]{1,0:T(8,128)S(1)} %bitcast.222, f32[1024,128]{1,0:T(8,128)S(1)} %get-tuple-element.110), kind=kOutput, calls=%fused_computation.131 | convolution fusion | flops 1811939328 | bytes 5832704 | tf_op jit(solution)/shard_map/dot_general | solution.py:116
  109.4 8.7 %fusion.30 = f32[1152,128]{1,0:T(8,128)} fusion(f32[1024,1152]{1,0:T(8,128)S(1)} %bitcast.220, f32[1024,128]{1,0:T(8,128)S(1)} %get-tuple-element.110), kind=kOutput, calls=%fused_computation.132 | convolution fusion | flops 1811939328 | bytes 5832704 | tf_op jit(solution)/shard_map/dot_general | solution.py:116
  118.2 8.6 %fusion.31 = f32[1152,128]{1,0:T(8,128)} fusion(f32[1024,1152]{1,0:T(8,128)S(1)} %bitcast.218, f32[1024,128]{1,0:T(8,128)S(1)} %get-tuple-element.110), kind=kOutput, calls=%fused_computation.133 | convolution fusion | flops 1811939328 | bytes 5832704 | tf_op jit(solution)/shard_map/dot_general | solution.py:116
  126.7 4.2 %fusion.5 = f32[2,8,8,8,9,128]{5,3,2,1,0,4:T(8,128)S(1)} fusion(f32[2,8,8,8,128,1]{4,3,2,1,0,5:T(8,128)S(1)} %bitcast.214, f32[27,128,128]{2,1,0:T(8,128)S(1)} %copy-done.2), kind=kOutput, calls=%fused_computation.17 | convolution fusion | flops 1811939328 | bytes 5832704 | tf_op jit(solution)/shard_map/dot_general | solution.py:126
  131.0 3.8 fusion.3
  134.8 4.0 fusion.7
  139.5 0.7 slice_bitcast_fusion.17
  140.2 1.0 slice_bitcast_fusion.8
  141.2 2.9 pad_add_fusion
  144.1 1.1 reshape.431
  145.2 12.2 %scatter_custom_fusion.3 = f32[2560,128]{1,0:T(8,128)S(1)} fusion(s32[2000]{0:T(1024)S(1)} %bitcast.244, f32[2000,128]{1,0:T(8,128)} %reshape.431, f32[]{:T(128)} %constant.74.clone.1), kind=kCustom, calls=%fused_computation.13 | custom fusion | flops 256000 | bytes 1311232 | tf_op jit(solution)/shard_map/scatter-add | solution.py:143
  157.4 1.9 collective-permute-start.2
  159.4 5.9 %collective-permute-start.3 = (f32[1,1,512,128]{3,2,1,0:T(8,128)S(1)}, f32[1,1,512,128]{3,2,1,0:T(8,128)S(1)}, u32[]{:S(2)}, u32[]{:S(2)}) collective-permute-start(f32[1,1,512,128]{3,2,1,0:T(8,128)S(1)} %get-tuple-element.108), channel_id=1, source_target_pairs={{8,0},{16,8},{24,16},{32,24},{40,32},{48,40},{56,48},{64,56},{72,6... | collective-permute-start | bytes 786440 | tf_op jit(solution)/shard_map/ppermute | solution.py:25
  165.3 1.4 pad_maximum_fusion
  166.7 0.7 collective-permute-done.2
  167.4 0.7 fusion.12
  168.1 1.0 collective-permute-done.3
  169.2 0.7 fusion.13
  169.9 4.0 gather_fusion.2
  174.0 10.4 %all-to-all-start.2 = ((f32[64,16,128]{2,1,0:T(8,128)}), f32[64,16,128]{2,1,0:T(8,128)S(1)}, u32[]{:S(2)}, u32[]{:S(2)}) async-start(f32[64,16,128]{2,1,0:T(8,128)} %bitcast.231), calls=%async_computation.2 | async-start | bytes 1048576 | tf_op jit(solution)/shard_map/all_to_all | solution.py:158
  184.3 123.3 %fusion = f32[64,128]{1,0:T(8,128)S(1)} fusion(f32[3456,128]{1,0:T(8,128)S(1)} %pad_maximum_fusion), kind=kCustom, calls=%all-reduce-scatter | all-reduce-scatter fusion | flops 524289 | bytes 1804288
  307.6 1.9 collective-permute-start.10
  309.5 4.5 %collective-permute-start.11 = (f32[64,128]{1,0:T(8,128)S(1)}, f32[64,128]{1,0:T(8,128)S(1)}, u32[]{:S(2)}, u32[]{:S(2)}) collective-permute-start(f32[64,128]{1,0:T(8,128)S(1)} %fusion), channel_id=1, source_target_pairs={{0,64},{8,72},{16,80},{24,88},{32,96},{40,104},{48,112},{56,120},{... | collective-permute-start | bytes 98312
  314.0 8.4 %collective-permute-start.12 = (f32[64,128]{1,0:T(8,128)S(1)}, f32[64,128]{1,0:T(8,128)S(1)}, u32[]{:S(2)}, u32[]{:S(2)}) collective-permute-start(f32[64,128]{1,0:T(8,128)S(1)} %fusion), channel_id=1, source_target_pairs={{0,72},{8,80},{16,88},{24,96},{32,104},{40,112},{48,120},{56,128},... | collective-permute-start | bytes 98312
  322.4 2.1 collective-permute-start.4
  324.5 10.3 %collective-permute-start.13 = (f32[54,128]{1,0:T(8,128)S(1)}, f32[54,128]{1,0:T(8,128)S(1)}, u32[]{:S(2)}, u32[]{:S(2)}) collective-permute-start(f32[54,128]{1,0:T(8,128)S(1)} %slice.419), channel_id=1, source_target_pairs={{0,80},{8,88},{16,96},{24,104},{32,112},{40,120},{48,128},{56,136}... | collective-permute-start | bytes 82952
  334.8 1.5 collective-permute-done.13
  336.3 7.7 %collective-permute-start.5 = (f32[64,128]{1,0:T(8,128)S(1)}, f32[64,128]{1,0:T(8,128)S(1)}, u32[]{:S(2)}, u32[]{:S(2)}) collective-permute-start(f32[64,128]{1,0:T(8,128)S(1)} %fusion), channel_id=1, source_target_pairs={{0,16},{8,24},{16,32},{24,40},{32,48},{40,56},{48,64},{56,72},{64,... | collective-permute-start | bytes 98312
  344.1 9.3 %collective-permute-start.6 = (f32[64,128]{1,0:T(8,128)S(1)}, f32[64,128]{1,0:T(8,128)S(1)}, u32[]{:S(2)}, u32[]{:S(2)}) collective-permute-start(f32[64,128]{1,0:T(8,128)S(1)} %fusion), channel_id=1, source_target_pairs={{0,24},{8,32},{16,40},{24,48},{32,56},{40,64},{48,72},{56,80},{64,... | collective-permute-start | bytes 98312
  353.4 3.1 collective-permute-start.7
  356.5 1.9 collective-permute-start.8
  358.4 3.1 collective-permute-start.9
  361.6 1.3 dynamic-slice.32
  363.5 2.8 collective-permute-done.8
  366.3 2.8 collective-permute-done.9
  369.2 1.6 concatenate.39
  370.8 30.4 %psum.7 = f32[54,128]{1,0:T(8,128)S(1)} all-reduce(f32[54,128]{1,0:T(8,128)S(1)} %constant_dynamic-slice_fusion), channel_id=1, replica_groups=mesh['slab'=64,'dp'=8] {'dp'}, use_global_device_ids=true, to_apply=%region_10.11 | all-reduce | flops 6912 | bytes 55296 | tf_op jit(solution)/shard_map/psum | solution.py:161
  401.8 1.6 gather_fusion.3
  (67 shorter events, 5.3 us)
Async XLA Ops:
  0.6 31.6 %copy-start = (f32[1,512,128]{2,1,0:T(8,128)S(1)}, f32[1,512,128]{2,1,0:T(8,128)}, u32[]{:S(2)}) copy-start(f32[1,512,128]{2,1,0:T(8,128)} %param.14) | copy-start | bytes 786436
  0.6 45.9 %copy-start.9 = (s32[1000]{0:T(1024)S(1)}, s32[1000]{0:T(1024)}, u32[]{:S(2)}) copy-start(s32[1000]{0:T(1024)} %constant.196) | copy-start | bytes 12004
  0.7 49.0 %copy-start.8 = (s32[1000]{0:T(1024)S(1)}, s32[1000]{0:T(1024)}, u32[]{:S(2)}) copy-start(s32[1000]{0:T(1024)} %constant.90.clone) | copy-start | bytes 12004
  8.2 26.6 %all-to-all-start = ((s32[64,1,16]{2,1,0:T(1,128)}), s32[64,1,16]{2,1,0:T(1,128)S(1)}, u32[]{:S(2)}, u32[]{:S(2)}) async-start(s32[64,1,16]{2,1,0:T(1,128)} %bitcast.7), calls=%async_computation | async-start | bytes 65536 | tf_op jit(solution)/shard_map/all_to_all | solution.py:74
  34.9 27.0 %all-to-all-start.1 = ((f32[64,16,128]{2,1,0:T(8,128)}), f32[64,16,128]{2,1,0:T(8,128)S(1)}, u32[]{:S(2)}, u32[]{:S(2)}) async-start(f32[64,16,128]{2,1,0:T(8,128)} %bitcast.10), calls=%async_computation.1 | async-start | bytes 1048576 | tf_op jit(solution)/shard_map/all_to_all | solution.py:71
  68.2 9.8 %collective-permute-start = (f32[1,1,512,128]{3,2,1,0:T(8,128)S(1)}, f32[1,1,512,128]{3,2,1,0:T(8,128)S(1)}, u32[]{:S(2)}, u32[]{:S(2)}) collective-permute-start(f32[1,1,512,128]{3,2,1,0:T(8,128)S(1)} %get-tuple-element.112), channel_id=1, source_target_pairs={{0,8},{8,16},{16,24},{24,32},{32,40},{40,48},{48,56},{56,64},{64,7... | collective-permute-start | bytes 786440 | tf_op jit(solution)/shard_map/ppermute | solution.py:24
  70.6 9.1 %collective-permute-start.1 = (f32[1,1,512,128]{3,2,1,0:T(8,128)S(1)}, f32[1,1,512,128]{3,2,1,0:T(8,128)S(1)}, u32[]{:S(2)}, u32[]{:S(2)}) collective-permute-start(f32[1,1,512,128]{3,2,1,0:T(8,128)S(1)} %get-tuple-element.113), channel_id=1, source_target_pairs={{8,0},{16,8},{24,16},{32,24},{40,32},{48,40},{56,48},{64,56},{72,6... | collective-permute-start | bytes 786440 | tf_op jit(solution)/shard_map/ppermute | solution.py:25
  87.0 1.1 copy-start.6
  87.4 4.8 %copy-start.5 = (f32[9,128,128]{2,1,0:T(8,128)S(1)}, f32[9,128,128]{2,1,0:T(8,128)}, u32[]{:S(2)}) copy-start(f32[9,128,128]{2,1,0:T(8,128)} %get-tuple-element.80) | copy-start | bytes 1769476
  88.1 8.2 %copy-start.4 = (f32[9,128,128]{2,1,0:T(8,128)S(1)}, f32[9,128,128]{2,1,0:T(8,128)}, u32[]{:S(2)}) copy-start(f32[9,128,128]{2,1,0:T(8,128)} %get-tuple-element.78) | copy-start | bytes 1769476
  88.1 8.2 %copy-start.7 = (f32[1,1024,128]{2,1,0:T(8,128)S(1)}, f32[1,1024,128]{2,1,0:T(8,128)}, u32[]{:S(2)}) copy-start(f32[1,1024,128]{2,1,0:T(8,128)} %param.21) | copy-start | bytes 1572868
  109.4 17.3 %copy-start.2 = (f32[27,128,128]{2,1,0:T(8,128)S(1)}, f32[27,128,128]{2,1,0:T(8,128)}, u32[]{:S(2)}) copy-start(f32[27,128,128]{2,1,0:T(8,128)} %param.20) | copy-start | bytes 5308420
  157.4 2.0 copy-start.3
  157.4 10.0 %collective-permute-start.2 = (f32[1,1,512,128]{3,2,1,0:T(8,128)S(1)}, f32[1,1,512,128]{3,2,1,0:T(8,128)S(1)}, u32[]{:S(2)}, u32[]{:S(2)}) collective-permute-start(f32[1,1,512,128]{3,2,1,0:T(8,128)S(1)} %get-tuple-element.109), channel_id=1, source_target_pairs={{0,8},{8,16},{16,24},{24,32},{32,40},{40,48},{48,56},{56,64},{64,7... | collective-permute-start | bytes 786440 | tf_op jit(solution)/shard_map/ppermute | solution.py:24
  159.4 9.8 %collective-permute-start.3 = (f32[1,1,512,128]{3,2,1,0:T(8,128)S(1)}, f32[1,1,512,128]{3,2,1,0:T(8,128)S(1)}, u32[]{:S(2)}, u32[]{:S(2)}) collective-permute-start(f32[1,1,512,128]{3,2,1,0:T(8,128)S(1)} %get-tuple-element.108), channel_id=1, source_target_pairs={{8,0},{16,8},{24,16},{32,24},{40,32},{48,40},{56,48},{64,56},{72,6... | collective-permute-start | bytes 786440 | tf_op jit(solution)/shard_map/ppermute | solution.py:25
  165.3 2.1 slice-start
  169.9 233.5 %copy-start.1 = (f32[1,512,128]{2,1,0:T(8,128)S(1)}, f32[1,512,128]{2,1,0:T(8,128)}, u32[]{:S(2)}) copy-start(f32[1,512,128]{2,1,0:T(8,128)} %param.14) | copy-start | bytes 786436
  174.0 227.9 %all-to-all-start.2 = ((f32[64,16,128]{2,1,0:T(8,128)}), f32[64,16,128]{2,1,0:T(8,128)S(1)}, u32[]{:S(2)}, u32[]{:S(2)}) async-start(f32[64,16,128]{2,1,0:T(8,128)} %bitcast.231), calls=%async_computation.2 | async-start | bytes 1048576 | tf_op jit(solution)/shard_map/all_to_all | solution.py:158
  307.6 36.5 %collective-permute-start.10 = (f32[64,128]{1,0:T(8,128)S(1)}, f32[64,128]{1,0:T(8,128)S(1)}, u32[]{:S(2)}, u32[]{:S(2)}) collective-permute-start(f32[64,128]{1,0:T(8,128)S(1)} %fusion), channel_id=1, source_target_pairs={{0,56},{8,64},{16,72},{24,80},{32,88},{40,96},{48,104},{56,112},{6... | collective-permute-start | bytes 98312
  309.5 43.8 %collective-permute-start.11 = (f32[64,128]{1,0:T(8,128)S(1)}, f32[64,128]{1,0:T(8,128)S(1)}, u32[]{:S(2)}, u32[]{:S(2)}) collective-permute-start(f32[64,128]{1,0:T(8,128)S(1)} %fusion), channel_id=1, source_target_pairs={{0,64},{8,72},{16,80},{24,88},{32,96},{40,104},{48,112},{56,120},{... | collective-permute-start | bytes 98312
  314.0 42.5 %collective-permute-start.12 = (f32[64,128]{1,0:T(8,128)S(1)}, f32[64,128]{1,0:T(8,128)S(1)}, u32[]{:S(2)}, u32[]{:S(2)}) collective-permute-start(f32[64,128]{1,0:T(8,128)S(1)} %fusion), channel_id=1, source_target_pairs={{0,72},{8,80},{16,88},{24,96},{32,104},{40,112},{48,120},{56,128},... | collective-permute-start | bytes 98312
  322.4 36.0 %collective-permute-start.4 = (f32[64,128]{1,0:T(8,128)S(1)}, f32[64,128]{1,0:T(8,128)S(1)}, u32[]{:S(2)}, u32[]{:S(2)}) collective-permute-start(f32[64,128]{1,0:T(8,128)S(1)} %fusion), channel_id=1, source_target_pairs={{0,8},{8,16},{16,24},{24,32},{32,40},{40,48},{48,56},{56,64},{64,7... | collective-permute-start | bytes 98312
  324.5 11.8 %collective-permute-start.13 = (f32[54,128]{1,0:T(8,128)S(1)}, f32[54,128]{1,0:T(8,128)S(1)}, u32[]{:S(2)}, u32[]{:S(2)}) collective-permute-start(f32[54,128]{1,0:T(8,128)S(1)} %slice.419), channel_id=1, source_target_pairs={{0,80},{8,88},{16,96},{24,104},{32,112},{40,120},{48,128},{56,136}... | collective-permute-start | bytes 82952
  336.3 27.2 %collective-permute-start.5 = (f32[64,128]{1,0:T(8,128)S(1)}, f32[64,128]{1,0:T(8,128)S(1)}, u32[]{:S(2)}, u32[]{:S(2)}) collective-permute-start(f32[64,128]{1,0:T(8,128)S(1)} %fusion), channel_id=1, source_target_pairs={{0,16},{8,24},{16,32},{24,40},{32,48},{40,56},{48,64},{56,72},{64,... | collective-permute-start | bytes 98312
  344.1 19.4 %collective-permute-start.6 = (f32[64,128]{1,0:T(8,128)S(1)}, f32[64,128]{1,0:T(8,128)S(1)}, u32[]{:S(2)}, u32[]{:S(2)}) collective-permute-start(f32[64,128]{1,0:T(8,128)S(1)} %fusion), channel_id=1, source_target_pairs={{0,24},{8,32},{16,40},{24,48},{32,56},{40,64},{48,72},{56,80},{64,... | collective-permute-start | bytes 98312
  353.4 10.1 %collective-permute-start.7 = (f32[64,128]{1,0:T(8,128)S(1)}, f32[64,128]{1,0:T(8,128)S(1)}, u32[]{:S(2)}, u32[]{:S(2)}) collective-permute-start(f32[64,128]{1,0:T(8,128)S(1)} %fusion), channel_id=1, source_target_pairs={{0,32},{8,40},{16,48},{24,56},{32,64},{40,72},{48,80},{56,88},{64,... | collective-permute-start | bytes 98312
  356.5 9.9 %collective-permute-start.8 = (f32[64,128]{1,0:T(8,128)S(1)}, f32[64,128]{1,0:T(8,128)S(1)}, u32[]{:S(2)}, u32[]{:S(2)}) collective-permute-start(f32[64,128]{1,0:T(8,128)S(1)} %fusion), channel_id=1, source_target_pairs={{0,40},{8,48},{16,56},{24,64},{32,72},{40,80},{48,88},{56,96},{64,... | collective-permute-start | bytes 98312
  358.4 10.8 %collective-permute-start.9 = (f32[64,128]{1,0:T(8,128)S(1)}, f32[64,128]{1,0:T(8,128)S(1)}, u32[]{:S(2)}, u32[]{:S(2)}) collective-permute-start(f32[64,128]{1,0:T(8,128)S(1)} %fusion), channel_id=1, source_target_pairs={{0,48},{8,56},{16,64},{24,72},{32,80},{40,88},{48,96},{56,104},{64... | collective-permute-start | bytes 98312
where the time goes:
time: 411 us; the launch traced here: 404 us
  blocking collectives  154 us (37%)
  starting transfers between devices  102 us (25%)
  matrix products  50.7 us (12%)
  local copies, waits for them, and re-layouts  34.7 us (8%)
  other arithmetic  31.4 us (8%)
  waiting for transfers between devices  24.8 us (6%)
  between operations  6.27 us (2%)
    unnamed x1, blocking collectives  123 us
    unnamed x10, starting transfers between devices  52.3 us
    psum x1, blocking collectives, per_device(): total = lax.psum(share, 'dp')  30.4 us
    dot_general x3, matrix products, per_device(): lax.dot_general(columns, grad_pre, (((0,), (0,)), ((), ())), precision=hi...  25 us
    all_to_all x1, starting transfers between devices, per_device(): lax.all_to_all(send_ids.reshape(slabs, capacity), 'slab', split_axis=0, c...  13.9 us
    dot_general x3, matrix products, per_device(): jnp.dot(columns, group_weight, precision=highest, preferred_element_type=...  13.6 us
    scatter-add x1, other arithmetic, per_device(): grad_visible = jnp.zeros((slots_all * VOX, C), jnp.float32).at[gather_row...  12.2 us
    dot_general x3, matrix products, per_device(): jnp.dot(grad_pre, group_back, precision=highest, preferred_element_type=j...  12.1 us
  transfers between devices with their start and end apart: 17, of which 8 were waited for; matrix products, arithmetic and copies ran while one was open for 35% of the time, Pallas kernels for 0%

commit v1 on v0

--- a/solution.py
+++ b/solution.py
@@ -158,7 +158,10 @@
     came_back = lax.all_to_all(back_points, "slab", split_axis=0, concat_axis=0, tiled=True)
     point_grads = came_back.reshape(slabs * capacity, C)[placement]
     share = lax.psum_scatter(weight_term, "slab", scatter_dimension=0, tiled=True)
-    total = lax.psum(share, "dp")
+    n_dev, total = (lax.axis_size("dp"), share)
+    for reach in [1 << k for k in range(n_dev.bit_length() - 1)]:
+        swap = [(i_2, i_2 ^ reach) for i_2 in range(n_dev)]
+        total = total + lax.ppermute(total, "dp", swap)
     scale = 1.0 / math.sqrt(windows * slabs * NB * VOX)
     return (activated[None], point_grads[None], total * scale)
 

time: 411 us -> 402 us (0.978)
  the two profiles are of different devices: /device:TPU:4 before, /device:TPU:44 now
where the time goes in v1:
time: 402 us; the launch traced here: 395 us
  blocking collectives  123 us (31%)
  starting transfers between devices  111 us (28%)
  matrix products  50.7 us (13%)
  waiting for transfers between devices  36.9 us (9%)
  local copies, waits for them, and re-layouts  34.8 us (9%)
  other arithmetic  31.3 us (8%)
  between operations  6.29 us (2%)
    unnamed x1, blocking collectives  123 us
    unnamed x10, starting transfers between devices  52.6 us
    dot_general x3, matrix products, per_device(): lax.dot_general(columns, grad_pre, (((0,), (0,)), ((), ())), precision=hi...  25 us
    all_to_all x1, starting transfers between devices, per_device(): lax.all_to_all(send_ids.reshape(slabs, capacity), 'slab', split_axis=0, c...  13.9 us
    ppermute x3, waiting for transfers between devices, per_device(): total = total + lax.ppermute(total, 'dp', swap)  13.7 us
    dot_general x3, matrix products, per_device(): jnp.dot(columns, group_weight, precision=highest, preferred_element_type=...  13.6 us
    scatter-add x1, other arithmetic, per_device(): grad_visible = jnp.zeros((slots_all * VOX, C), jnp.float32).at[gather_row...  12.2 us
    dot_general x3, matrix products, per_device(): jnp.dot(grad_pre, group_back, precision=highest, preferred_element_type=j...  12.1 us
  transfers between devices with their start and end apart: 20, of which 11 were waited for; matrix products, arithmetic and copies ran while one was open for 36% of the time, Pallas kernels for 0%

profile of v1, /device:TPU:44, one launch (start us, length us, event | category | flops | bytes accessed | tf_op | source)
XLA Modules:
  0.0 394.7 jit_solution(10436642978822661147)
XLA Ops:
  0.7 0.7 fusion.20
  1.4 1.2 reduce-window.6
  2.9 0.8 fusion.19
  3.7 0.7 compare_select_fusion.4
  4.4 0.7 multiply_add_fusion
  5.1 2.4 scatter_custom_fusion
  8.2 13.9 %all-to-all-start = ((s32[64,1,16]{2,1,0:T(1,128)}), s32[64,1,16]{2,1,0:T(1,128)S(1)}, u32[]{:S(2)}, u32[]{:S(2)}) async-start(s32[64,1,16]{2,1,0:T(1,128)} %bitcast.7), calls=%async_computation | async-start | bytes 65536 | tf_op jit(solution)/shard_map/all_to_all | solution.py:74
  22.2 1.3 fusion.27
  26.1 2.7 fusion.26
  30.1 1.4 and_reduce_fusion
  31.5 0.8 copy.103
  32.3 2.5 scatter_custom_fusion.1
  34.9 10.3 %all-to-all-start.1 = ((f32[64,16,128]{2,1,0:T(8,128)}), f32[64,16,128]{2,1,0:T(8,128)S(1)}, u32[]{:S(2)}, u32[]{:S(2)}) async-start(f32[64,16,128]{2,1,0:T(8,128)} %bitcast.10), calls=%async_computation.1 | async-start | bytes 1048576 | tf_op jit(solution)/shard_map/all_to_all | solution.py:71
  45.7 0.7 reduce.21
  46.6 2.9 gather_fusion
  49.8 12.1 %all-to-all-done.1 = f32[64,16,128]{2,1,0:T(8,128)S(1)} async-done(((f32[64,16,128]{2,1,0:T(8,128)}), f32[64,16,128]{2,1,0:T(8,128)S(1)}, u32[]{:S(2)}, u32[]{:S(2)}) %all-to-all-start.1) | async-done | bytes 524320 | tf_op jit(solution)/shard_map/all_to_all | solution.py:71
  61.9 6.2 %scatter_custom_fusion.2 = f32[1025,128]{1,0:T(8,128)S(1)} fusion(s32[1024]{0:T(1024)S(1)} %bitcast.239, f32[1024,128]{1,0:T(8,128)S(1)} %bitcast.232, f32[]{:T(128)} %constant.74.clone.1), kind=kCustom, calls=%fused_computation.81 | custom fusion | flops 131072 | bytes 524804 | tf_op jit(solution)/shard_map/scatter-add | solution.py:83
  68.2 2.4 collective-permute-start
  70.6 5.2 %collective-permute-start.1 = (f32[1,1,512,128]{3,2,1,0:T(8,128)S(1)}, f32[1,1,512,128]{3,2,1,0:T(8,128)S(1)}, u32[]{:S(2)}, u32[]{:S(2)}) collective-permute-start(f32[1,1,512,128]{3,2,1,0:T(8,128)S(1)} %get-tuple-element.113), channel_id=1, source_target_pairs={{8,0},{16,8},{24,16},{32,24},{40,32},{48,40},{56,48},{64,56},{72,6... | collective-permute-start | bytes 786440 | tf_op jit(solution)/shard_map/ppermute | solution.py:25
  76.0 2.0 collective-permute-done
  78.0 1.8 collective-permute-done.1
  79.9 5.8 %gather_fusion.1 = f32[2000,128]{1,0:T(8,128)S(1)} fusion(f32[2560,128]{1,0:T(8,128)S(1)} %bitcast.213, s32[2048]{0:T(1024)S(1)} %pad_clamp_fusion), kind=kCustom, calls=%fused_computation.1 | custom fusion | bytes 2056000 | tf_op jit(solution)/shard_map/gather | solution.py:100
  88.1 4.1 %fusion.28 = f32[1024,128]{1,0:T(8,128)S(1)} fusion(f32[1024,1152]{1,0:T(8,128)S(1)} %bitcast.221, f32[1152,128]{1,0:T(8,128)S(1)} %bitcast.230), kind=kOutput, calls=%fused_computation.130 | convolution fusion | flops 1811939328 | bytes 5832704 | tf_op jit(solution)/shard_map/dot_general | solution.py:105
  92.2 4.1 %convolution_add_fusion.1 = f32[1024,128]{1,0:T(8,128)S(1)} fusion(f32[1024,128]{1,0:T(8,128)S(1)} %fusion.28, f32[1024,1152]{1,0:T(8,128)S(1)} %bitcast.219, f32[1152,128]{1,0:T(8,128)S(1)} %bitcast.229), kind=kOutput, calls=%fused_computation.12 | convolution fusion | flops 1812070400 | bytes 6356992 | tf_op jit(solution)/shard_map/dot_general | solution.py:105
  96.3 5.4 %fusion.9 = (f32[1024,128]{1,0:T(8,128)S(1)}, f32[1,1024,128]{2,1,0:T(8,128)}) fusion(f32[1,1024,128]{2,1,0:T(8,128)S(1)} %copy-done.7, f32[1024,128]{1,0:T(8,128)S(1)} %convolution_add_fusion.1, f32[1024,1152]{1,0:T(8,128)S(1)} %bitcast.217, f32[1152,128]{1,0:T(8,128)S(1)} %bitcast.228), kind=kOutput, calls=%fused_computation.76 | convolution fusion | flops 1813250048 | bytes 7405568 | tf_op jit(solution)/shard_map/dot_general | solution.py:105
  101.7 7.7 %fusion.29 = f32[1152,128]{1,0:T(8,128)S(1)} fusion(f32[1024,1152]{1,0:T(8,128)S(1)} %bitcast.222, f32[1024,128]{1,0:T(8,128)S(1)} %get-tuple-element.110), kind=kOutput, calls=%fused_computation.131 | convolution fusion | flops 1811939328 | bytes 5832704 | tf_op jit(solution)/shard_map/dot_general | solution.py:116
  109.5 8.7 %fusion.30 = f32[1152,128]{1,0:T(8,128)} fusion(f32[1024,1152]{1,0:T(8,128)S(1)} %bitcast.220, f32[1024,128]{1,0:T(8,128)S(1)} %get-tuple-element.110), kind=kOutput, calls=%fused_computation.132 | convolution fusion | flops 1811939328 | bytes 5832704 | tf_op jit(solution)/shard_map/dot_general | solution.py:116
  118.2 8.5 %fusion.31 = f32[1152,128]{1,0:T(8,128)} fusion(f32[1024,1152]{1,0:T(8,128)S(1)} %bitcast.218, f32[1024,128]{1,0:T(8,128)S(1)} %get-tuple-element.110), kind=kOutput, calls=%fused_computation.133 | convolution fusion | flops 1811939328 | bytes 5832704 | tf_op jit(solution)/shard_map/dot_general | solution.py:116
  126.8 4.2 %fusion.5 = f32[2,8,8,8,9,128]{5,3,2,1,0,4:T(8,128)S(1)} fusion(f32[2,8,8,8,128,1]{4,3,2,1,0,5:T(8,128)S(1)} %bitcast.214, f32[27,128,128]{2,1,0:T(8,128)S(1)} %copy-done.2), kind=kOutput, calls=%fused_computation.17 | convolution fusion | flops 1811939328 | bytes 5832704 | tf_op jit(solution)/shard_map/dot_general | solution.py:126
  131.0 3.8 fusion.3
  134.9 4.0 %fusion.7 = f32[2,8,8,8,9,128]{5,3,4,2,1,0:T(8,128)S(1)} fusion(f32[2,8,8,8,128,1]{4,3,5,2,1,0:T(8,128)S(1)} %bitcast.216, f32[27,128,128]{2,1,0:T(8,128)S(1)} %copy-done.2), kind=kOutput, calls=%fused_computation.19 | convolution fusion | flops 1811939328 | bytes 5832704 | tf_op jit(solution)/shard_map/dot_general | solution.py:126
  140.2 1.0 slice_bitcast_fusion.8
  141.2 2.9 pad_add_fusion
  144.1 1.1 reshape.431
  145.2 12.2 %scatter_custom_fusion.3 = f32[2560,128]{1,0:T(8,128)S(1)} fusion(s32[2000]{0:T(1024)S(1)} %bitcast.244, f32[2000,128]{1,0:T(8,128)} %reshape.431, f32[]{:T(128)} %constant.74.clone.1), kind=kCustom, calls=%fused_computation.13 | custom fusion | flops 256000 | bytes 1311232 | tf_op jit(solution)/shard_map/scatter-add | solution.py:143
  157.5 1.9 collective-permute-start.2
  159.4 5.9 %collective-permute-start.3 = (f32[1,1,512,128]{3,2,1,0:T(8,128)S(1)}, f32[1,1,512,128]{3,2,1,0:T(8,128)S(1)}, u32[]{:S(2)}, u32[]{:S(2)}) collective-permute-start(f32[1,1,512,128]{3,2,1,0:T(8,128)S(1)} %get-tuple-element.108), channel_id=1, source_target_pairs={{8,0},{16,8},{24,16},{32,24},{40,32},{48,40},{56,48},{64,56},{72,6... | collective-permute-start | bytes 786440 | tf_op jit(solution)/shard_map/ppermute | solution.py:25
  165.3 1.4 pad_maximum_fusion
  167.4 0.7 fusion.12
  168.1 1.0 collective-permute-done.3
  169.8 4.0 %gather_fusion.2 = f32[1024,128]{1,0:T(8,128)} fusion(f32[1025,128]{1,0:T(8,128)S(1)} %concatenate.35, s32[1024]{0:T(1024)S(1)} %get-tuple-element.117), kind=kCustom, calls=%fused_computation.2 | custom fusion | bytes 1052672 | tf_op jit(solution)/shard_map/gather | solution.py:157
  173.9 10.3 %all-to-all-start.2 = ((f32[64,16,128]{2,1,0:T(8,128)}), f32[64,16,128]{2,1,0:T(8,128)S(1)}, u32[]{:S(2)}, u32[]{:S(2)}) async-start(f32[64,16,128]{2,1,0:T(8,128)} %bitcast.231), calls=%async_computation.2 | async-start | bytes 1048576 | tf_op jit(solution)/shard_map/all_to_all | solution.py:158
  184.2 123.3 %fusion = f32[64,128]{1,0:T(8,128)S(1)} fusion(f32[3456,128]{1,0:T(8,128)S(1)} %pad_maximum_fusion), kind=kCustom, calls=%all-reduce-scatter | all-reduce-scatter fusion | flops 524289 | bytes 1804288
  307.5 1.9 collective-permute-start.10
  309.4 1.9 collective-permute-start.11
  311.3 4.7 %collective-permute-start.12 = (f32[64,128]{1,0:T(8,128)S(1)}, f32[64,128]{1,0:T(8,128)S(1)}, u32[]{:S(2)}, u32[]{:S(2)}) collective-permute-start(f32[64,128]{1,0:T(8,128)S(1)} %fusion), channel_id=1, source_target_pairs={{0,48},{8,56},{16,64},{24,72},{32,80},{40,88},{48,96},{56,104},{64... | collective-permute-start | bytes 98312
  316.1 6.1 %collective-permute-start.13 = (f32[64,128]{1,0:T(8,128)S(1)}, f32[64,128]{1,0:T(8,128)S(1)}, u32[]{:S(2)}, u32[]{:S(2)}) collective-permute-start(f32[64,128]{1,0:T(8,128)S(1)} %fusion), channel_id=1, source_target_pairs={{0,56},{8,64},{16,72},{24,80},{32,88},{40,96},{48,104},{56,112},{6... | collective-permute-start | bytes 98312
  322.1 13.3 %collective-permute-start.16 = (f32[54,128]{1,0:T(8,128)S(1)}, f32[54,128]{1,0:T(8,128)S(1)}, u32[]{:S(2)}, u32[]{:S(2)}) collective-permute-start(f32[54,128]{1,0:T(8,128)S(1)} %slice.419), channel_id=1, source_target_pairs={{0,80},{8,88},{16,96},{24,104},{32,112},{40,120},{48,128},{56,136}... | collective-permute-start | bytes 82952
  335.4 1.8 collective-permute-done.16
  337.2 14.2 %collective-permute-start.14 = (f32[64,128]{1,0:T(8,128)S(1)}, f32[64,128]{1,0:T(8,128)S(1)}, u32[]{:S(2)}, u32[]{:S(2)}) collective-permute-start(f32[64,128]{1,0:T(8,128)S(1)} %fusion), channel_id=1, source_target_pairs={{0,64},{8,72},{16,80},{24,88},{32,96},{40,104},{48,112},{56,120},{... | collective-permute-start | bytes 98312
  351.5 1.9 collective-permute-start.15
  353.4 3.0 collective-permute-start.7
  356.4 3.1 collective-permute-start.8
  359.5 2.5 collective-permute-start.9
  362.0 1.3 dynamic-slice.32
  364.4 3.3 collective-permute-done.9
  367.8 1.6 concatenate.39
  369.4 3.2 collective-permute-start.4
  372.7 2.5 collective-permute-done.4
  375.2 2.7 collective-permute-start.5
  377.9 4.1 %collective-permute-done.5 = f32[54,128]{1,0:T(8,128)S(1)} collective-permute-done((f32[54,128]{1,0:T(8,128)S(1)}, f32[54,128]{1,0:T(8,128)S(1)}, u32[]{:S(2)}, u32[]{:S(2)}) %collective-permute-start.5) | collective-permute-done | bytes 27680 | tf_op jit(solution)/shard_map/ppermute | solution.py:164
  382.0 2.8 collective-permute-start.6
  384.8 7.1 %collective-permute-done.6 = f32[54,128]{1,0:T(8,128)S(1)} collective-permute-done((f32[54,128]{1,0:T(8,128)S(1)}, f32[54,128]{1,0:T(8,128)S(1)}, u32[]{:S(2)}, u32[]{:S(2)}) %collective-permute-start.6) | collective-permute-done | bytes 27680 | tf_op jit(solution)/shard_map/ppermute | solution.py:164
  392.6 1.6 gather_fusion.3
  (74 shorter events, 8.4 us)
Async XLA Ops:
  0.6 31.6 %copy-start = (f32[1,512,128]{2,1,0:T(8,128)S(1)}, f32[1,512,128]{2,1,0:T(8,128)}, u32[]{:S(2)}) copy-start(f32[1,512,128]{2,1,0:T(8,128)} %param.14) | copy-start | bytes 786436
  0.6 45.9 %copy-start.9 = (s32[1000]{0:T(1024)S(1)}, s32[1000]{0:T(1024)}, u32[]{:S(2)}) copy-start(s32[1000]{0:T(1024)} %constant.196) | copy-start | bytes 12004
  0.7 49.0 %copy-start.8 = (s32[1000]{0:T(1024)S(1)}, s32[1000]{0:T(1024)}, u32[]{:S(2)}) copy-start(s32[1000]{0:T(1024)} %constant.90.clone) | copy-start | bytes 12004
  8.2 26.6 %all-to-all-start = ((s32[64,1,16]{2,1,0:T(1,128)}), s32[64,1,16]{2,1,0:T(1,128)S(1)}, u32[]{:S(2)}, u32[]{:S(2)}) async-start(s32[64,1,16]{2,1,0:T(1,128)} %bitcast.7), calls=%async_computation | async-start | bytes 65536 | tf_op jit(solution)/shard_map/all_to_all | solution.py:74
  34.9 27.0 %all-to-all-start.1 = ((f32[64,16,128]{2,1,0:T(8,128)}), f32[64,16,128]{2,1,0:T(8,128)S(1)}, u32[]{:S(2)}, u32[]{:S(2)}) async-start(f32[64,16,128]{2,1,0:T(8,128)} %bitcast.10), calls=%async_computation.1 | async-start | bytes 1048576 | tf_op jit(solution)/shard_map/all_to_all | solution.py:71
  68.2 9.8 %collective-permute-start = (f32[1,1,512,128]{3,2,1,0:T(8,128)S(1)}, f32[1,1,512,128]{3,2,1,0:T(8,128)S(1)}, u32[]{:S(2)}, u32[]{:S(2)}) collective-permute-start(f32[1,1,512,128]{3,2,1,0:T(8,128)S(1)} %get-tuple-element.112), channel_id=1, source_target_pairs={{0,8},{8,16},{16,24},{24,32},{32,40},{40,48},{48,56},{56,64},{64,7... | collective-permute-start | bytes 786440 | tf_op jit(solution)/shard_map/ppermute | solution.py:24
  70.6 9.1 %collective-permute-start.1 = (f32[1,1,512,128]{3,2,1,0:T(8,128)S(1)}, f32[1,1,512,128]{3,2,1,0:T(8,128)S(1)}, u32[]{:S(2)}, u32[]{:S(2)}) collective-permute-start(f32[1,1,512,128]{3,2,1,0:T(8,128)S(1)} %get-tuple-element.113), channel_id=1, source_target_pairs={{8,0},{16,8},{24,16},{32,24},{40,32},{48,40},{56,48},{64,56},{72,6... | collective-permute-start | bytes 786440 | tf_op jit(solution)/shard_map/ppermute | solution.py:25
  87.0 1.1 copy-start.6
  87.4 4.8 %copy-start.5 = (f32[9,128,128]{2,1,0:T(8,128)S(1)}, f32[9,128,128]{2,1,0:T(8,128)}, u32[]{:S(2)}) copy-start(f32[9,128,128]{2,1,0:T(8,128)} %get-tuple-element.80) | copy-start | bytes 1769476
  88.1 8.2 %copy-start.4 = (f32[9,128,128]{2,1,0:T(8,128)S(1)}, f32[9,128,128]{2,1,0:T(8,128)}, u32[]{:S(2)}) copy-start(f32[9,128,128]{2,1,0:T(8,128)} %get-tuple-element.78) | copy-start | bytes 1769476
  88.1 8.2 %copy-start.7 = (f32[1,1024,128]{2,1,0:T(8,128)S(1)}, f32[1,1024,128]{2,1,0:T(8,128)}, u32[]{:S(2)}) copy-start(f32[1,1024,128]{2,1,0:T(8,128)} %param.21) | copy-start | bytes 1572868
  109.5 17.3 %copy-start.2 = (f32[27,128,128]{2,1,0:T(8,128)S(1)}, f32[27,128,128]{2,1,0:T(8,128)}, u32[]{:S(2)}) copy-start(f32[27,128,128]{2,1,0:T(8,128)} %param.20) | copy-start | bytes 5308420
  157.4 2.0 copy-start.3
  157.5 10.0 %collective-permute-start.2 = (f32[1,1,512,128]{3,2,1,0:T(8,128)S(1)}, f32[1,1,512,128]{3,2,1,0:T(8,128)S(1)}, u32[]{:S(2)}, u32[]{:S(2)}) collective-permute-start(f32[1,1,512,128]{3,2,1,0:T(8,128)S(1)} %get-tuple-element.109), channel_id=1, source_target_pairs={{0,8},{8,16},{16,24},{24,32},{32,40},{40,48},{48,56},{56,64},{64,7... | collective-permute-start | bytes 786440 | tf_op jit(solution)/shard_map/ppermute | solution.py:24
  159.4 9.8 %collective-permute-start.3 = (f32[1,1,512,128]{3,2,1,0:T(8,128)S(1)}, f32[1,1,512,128]{3,2,1,0:T(8,128)S(1)}, u32[]{:S(2)}, u32[]{:S(2)}) collective-permute-start(f32[1,1,512,128]{3,2,1,0:T(8,128)S(1)} %get-tuple-element.108), channel_id=1, source_target_pairs={{8,0},{16,8},{24,16},{32,24},{40,32},{48,40},{56,48},{64,56},{72,6... | collective-permute-start | bytes 786440 | tf_op jit(solution)/shard_map/ppermute | solution.py:25
  165.3 2.1 slice-start
  169.8 224.4 %copy-start.1 = (f32[1,512,128]{2,1,0:T(8,128)S(1)}, f32[1,512,128]{2,1,0:T(8,128)}, u32[]{:S(2)}) copy-start(f32[1,512,128]{2,1,0:T(8,128)} %param.14) | copy-start | bytes 786436
  173.9 218.7 %all-to-all-start.2 = ((f32[64,16,128]{2,1,0:T(8,128)}), f32[64,16,128]{2,1,0:T(8,128)S(1)}, u32[]{:S(2)}, u32[]{:S(2)}) async-start(f32[64,16,128]{2,1,0:T(8,128)} %bitcast.231), calls=%async_computation.2 | async-start | bytes 1048576 | tf_op jit(solution)/shard_map/all_to_all | solution.py:158
  307.5 44.0 %collective-permute-start.10 = (f32[64,128]{1,0:T(8,128)S(1)}, f32[64,128]{1,0:T(8,128)S(1)}, u32[]{:S(2)}, u32[]{:S(2)}) collective-permute-start(f32[64,128]{1,0:T(8,128)S(1)} %fusion), channel_id=1, source_target_pairs={{0,32},{8,40},{16,48},{24,56},{32,64},{40,72},{48,80},{56,88},{64,... | collective-permute-start | bytes 98312
  309.4 44.0 %collective-permute-start.11 = (f32[64,128]{1,0:T(8,128)S(1)}, f32[64,128]{1,0:T(8,128)S(1)}, u32[]{:S(2)}, u32[]{:S(2)}) collective-permute-start(f32[64,128]{1,0:T(8,128)S(1)} %fusion), channel_id=1, source_target_pairs={{0,40},{8,48},{16,56},{24,64},{32,72},{40,80},{48,88},{56,96},{64,... | collective-permute-start | bytes 98312
  311.3 45.1 %collective-permute-start.12 = (f32[64,128]{1,0:T(8,128)S(1)}, f32[64,128]{1,0:T(8,128)S(1)}, u32[]{:S(2)}, u32[]{:S(2)}) collective-permute-start(f32[64,128]{1,0:T(8,128)S(1)} %fusion), channel_id=1, source_target_pairs={{0,48},{8,56},{16,64},{24,72},{32,80},{40,88},{48,96},{56,104},{64... | collective-permute-start | bytes 98312
  316.1 43.4 %collective-permute-start.13 = (f32[64,128]{1,0:T(8,128)S(1)}, f32[64,128]{1,0:T(8,128)S(1)}, u32[]{:S(2)}, u32[]{:S(2)}) collective-permute-start(f32[64,128]{1,0:T(8,128)S(1)} %fusion), channel_id=1, source_target_pairs={{0,56},{8,64},{16,72},{24,80},{32,88},{40,96},{48,104},{56,112},{6... | collective-permute-start | bytes 98312
  322.1 15.1 %collective-permute-start.16 = (f32[54,128]{1,0:T(8,128)S(1)}, f32[54,128]{1,0:T(8,128)S(1)}, u32[]{:S(2)}, u32[]{:S(2)}) collective-permute-start(f32[54,128]{1,0:T(8,128)S(1)} %slice.419), channel_id=1, source_target_pairs={{0,80},{8,88},{16,96},{24,104},{32,112},{40,120},{48,128},{56,136}... | collective-permute-start | bytes 82952
  337.2 26.7 %collective-permute-start.14 = (f32[64,128]{1,0:T(8,128)S(1)}, f32[64,128]{1,0:T(8,128)S(1)}, u32[]{:S(2)}, u32[]{:S(2)}) collective-permute-start(f32[64,128]{1,0:T(8,128)S(1)} %fusion), channel_id=1, source_target_pairs={{0,64},{8,72},{16,80},{24,88},{32,96},{40,104},{48,112},{56,120},{... | collective-permute-start | bytes 98312
  351.5 12.5 %collective-permute-start.15 = (f32[64,128]{1,0:T(8,128)S(1)}, f32[64,128]{1,0:T(8,128)S(1)}, u32[]{:S(2)}, u32[]{:S(2)}) collective-permute-start(f32[64,128]{1,0:T(8,128)S(1)} %fusion), channel_id=1, source_target_pairs={{0,72},{8,80},{16,88},{24,96},{32,104},{40,112},{48,120},{56,128},... | collective-permute-start | bytes 98312
  353.4 10.6 %collective-permute-start.7 = (f32[64,128]{1,0:T(8,128)S(1)}, f32[64,128]{1,0:T(8,128)S(1)}, u32[]{:S(2)}, u32[]{:S(2)}) collective-permute-start(f32[64,128]{1,0:T(8,128)S(1)} %fusion), channel_id=1, source_target_pairs={{0,8},{8,16},{16,24},{24,32},{32,40},{40,48},{48,56},{56,64},{64,7... | collective-permute-start | bytes 98312
  356.4 8.0 %collective-permute-start.8 = (f32[64,128]{1,0:T(8,128)S(1)}, f32[64,128]{1,0:T(8,128)S(1)}, u32[]{:S(2)}, u32[]{:S(2)}) collective-permute-start(f32[64,128]{1,0:T(8,128)S(1)} %fusion), channel_id=1, source_target_pairs={{0,16},{8,24},{16,32},{24,40},{32,48},{40,56},{48,64},{56,72},{64,... | collective-permute-start | bytes 98312
  359.5 8.3 %collective-permute-start.9 = (f32[64,128]{1,0:T(8,128)S(1)}, f32[64,128]{1,0:T(8,128)S(1)}, u32[]{:S(2)}, u32[]{:S(2)}) collective-permute-start(f32[64,128]{1,0:T(8,128)S(1)} %fusion), channel_id=1, source_target_pairs={{0,24},{8,32},{16,40},{24,48},{32,56},{40,64},{48,72},{56,80},{64,... | collective-permute-start | bytes 98312
  369.4 5.8 %collective-permute-start.4 = (f32[54,128]{1,0:T(8,128)S(1)}, f32[54,128]{1,0:T(8,128)S(1)}, u32[]{:S(2)}, u32[]{:S(2)}) collective-permute-start(f32[54,128]{1,0:T(8,128)S(1)} %constant_dynamic-slice_fusion), channel_id=1, source_target_pairs={{0,1},{1,0},{2,3},{3,2},{4,5},{5,4},{6,7},{7,6},{8,9},{9,8},{10,11... | collective-permute-start | bytes 82952 | tf_op jit(solution)/shard_map/ppermute | solution.py:164
  375.2 6.8 %collective-permute-start.5 = (f32[54,128]{1,0:T(8,128)S(1)}, f32[54,128]{1,0:T(8,128)S(1)}, u32[]{:S(2)}, u32[]{:S(2)}) collective-permute-start(f32[54,128]{1,0:T(8,128)S(1)} %fusion.47), channel_id=1, source_target_pairs={{0,2},{1,3},{2,0},{3,1},{4,6},{5,7},{6,4},{7,5},{8,10},{9,11},{10,... | collective-permute-start | bytes 82952 | tf_op jit(solution)/shard_map/ppermute | solution.py:164
  382.0 10.0 %collective-permute-start.6 = (f32[54,128]{1,0:T(8,128)S(1)}, f32[54,128]{1,0:T(8,128)S(1)}, u32[]{:S(2)}, u32[]{:S(2)}) collective-permute-start(f32[54,128]{1,0:T(8,128)S(1)} %add.335), channel_id=1, source_target_pairs={{0,4},{1,5},{2,6},{3,7},{4,0},{5,1},{6,2},{7,3},{8,12},{9,13},{10,... | collective-permute-start | bytes 82952 | tf_op jit(solution)/shard_map/ppermute | solution.py:164
